TPU v7x, 32 devices: a whole 2x2x4 slice. The times are simulated.
32 devices in a mesh: group: 2 (over x), adapter: 8 (over z, y), tensor: 2 (over core).
Axes of the slice: x: 2, y: 2, z: 4, core: 2. Of those that a mesh axis runs over, the one named last changes fastest.
Arguments:
- tokens: bfloat16 [768, 8192], P(('group', 'adapter'), 'tensor'), parts along dimension 0, may hold values from -6 to 6
- token_row_adapter: int32 [768, 1], P('group'), parts along dimension 0, may hold values from 0 to 7
- output_weight: bfloat16 [8192, 8192], P('tensor', 'adapter'), may hold values from -0.0625 to 0.0625
- down_weight: bfloat16 [16, 8192, 64], P(('group', 'adapter'), 'tensor'), parts along dimension 0, may hold values from -0.0625 to 0.0625
- up_weight: bfloat16 [16, 64, 8192], P('group', 'tensor', 'adapter'), parts along dimension 0, may hold values from -0.75 to 0.75
Outputs:
- projected: bfloat16 [768, 8192], P('group', 'adapter'), parts along dimension 0
There are 2 independent parts, one for each index of `group`. A program takes and returns all parts, laid end to end along the dimension named above; an argument that names none is the same for every part. Nothing has to cross between parts.
Inputs may be any that keep to these rules, and one draw needn't show every extreme that they name: `token_row_adapter`: each adapter is named by at least one row.
All inputs are finite; a program needn't handle non-finite values.
Results may differ from a plain program's by a relative error of at most 0.011.
Values may be sent and summed in bfloat16 or wider, within the bound.
A program may use at most 128 MiB of HBM per device.

v0:
```python
import jax
import jax.numpy as jnp
from jax import lax
from jax.sharding import PartitionSpec as P

adapter_scale = 2.0


def local(tokens, token_row_adapter, output_weight, down_weight, up_weight):
    flat_ids = token_row_adapter[:, 0]
    tok_rows = tokens.shape[0]
    total_rows = flat_ids.shape[0]
    adapter_table = up_weight.shape[0]
    half_of_rank = up_weight.shape[1]
    output_columns = output_weight.shape[1]
    merged_output = jnp.dot(
        lax.all_gather(tokens, "adapter", axis=0, tiled=True),
        output_weight,
        preferred_element_type=jnp.float32,
    )
    own_ids = lax.dynamic_slice_in_dim(flat_ids, lax.axis_index("adapter") * tok_rows, tok_rows, 0)
    row_slice = lax.all_gather(down_weight, "adapter", axis=0, tiled=True)
    piece_adapters = jnp.arange(row_slice.shape[0], dtype=jnp.int32)
    rows_projected = jnp.einsum(
        "td,kdr->tkr", tokens, row_slice, preferred_element_type=jnp.float32
    )
    chosen = (own_ids[:, None] == piece_adapters[None, :]).astype(jnp.float32)
    own_low = jnp.einsum("tk,tkr->tr", chosen, rows_projected)
    own_low = lax.psum(own_low, "tensor").astype(jnp.bfloat16)
    low = lax.all_gather(own_low, "adapter", axis=0, tiled=True)
    low_half = lax.dynamic_slice_in_dim(
        low, lax.axis_index("tensor") * half_of_rank, half_of_rank, 1
    )
    onehot = (flat_ids[:, None] == jnp.arange(adapter_table, dtype=jnp.int32)[None, :]).astype(
        jnp.bfloat16
    )
    scattered_rows = (onehot[:, :, None] * low_half[:, None, :]).reshape(
        total_rows, adapter_table * half_of_rank
    )
    adapter_update = jnp.dot(
        scattered_rows,
        up_weight.reshape(adapter_table * half_of_rank, output_columns),
        preferred_element_type=jnp.float32,
    )
    partial_output = merged_output + adapter_scale * adapter_update
    summed = lax.psum(partial_output, "tensor")
    return summed.astype(jnp.bfloat16)


def solution(mesh):
    placed = (
        P(("group", "adapter"), "tensor"),
        P("group", None),
        P("tensor", "adapter"),
        P(("group", "adapter"), "tensor", None),
        P("group", "tensor", "adapter"),
    )
    return jax.shard_map(
        local, mesh=mesh, in_specs=placed, out_specs=P("group", "adapter"), check_vma=False
    )
```

profile of v0, /device:TPU:0, one launch (start us, length us, event | category | flops | bytes accessed | tf_op | source)
XLA Modules:
  0.0 202.2 jit_solution(12872553369827494276)
XLA Ops:
  6.5 0.0 copy-start
  6.5 0.0 all-gather.3.cloned.1.call-start
  6.5 0.7 all-gather.3.cloned.1.call-update
  7.3 0.0 all-gather.5.cloned.1.call-start
  7.3 0.7 all-gather.5.cloned.1.call-update
  8.0 0.7 reduce
  8.7 0.8 dynamic-slice_bitcast_fusion
  9.5 0.1 fusion.9
  9.6 0.0 copy-start.1
  9.6 63.2 %all-gather.3.cloned.1.call-done = bf16[384,4096]{1,0:T(8,128)(2,1)} async-done(((bf16[48,4096]{1,0:T(8,128)(2,1)}), bf16[384,4096]{1,0:T(8,128)(2,1)}) %all-gather.3.cloned.1.call-update) | async-done | bytes 3145744 | tf_op jit(solution)/shard_map/all_gather | solution.py:17
  72.7 9.0 %fusion.11 = f32[384,1024]{1,0:T(8,128)} fusion(bf16[384,4096]{1,0:T(8,128)(2,1)} %all-gather.3.cloned.1.call-done, bf16[4096,1024]{1,0:T(8,128)(2,1)} %param.7), kind=kOutput, calls=%fused_computation.16 | convolution fusion | flops 3221225472 | bytes 13107200 | tf_op jit(solution)/shard_map/dot_general | solution.py:16
  81.7 65.2 %all-gather.5.cloned.1.call-done = bf16[8,4096,64]{1,2,0:T(8,128)(2,1)} async-done(((bf16[1,4096,64]{1,2,0:T(8,128)(2,1)}), bf16[8,4096,64]{1,2,0:T(8,128)(2,1)}) %all-gather.5.cloned.1.call-update) | async-done | bytes 4194320 | tf_op jit(solution)/shard_map/all_gather | solution.py:22
  146.9 0.0 copy-done.1
  146.9 4.3 %fusion.1 = bf16[48,8,64]{2,0,1:T(8,128)(2,1)S(1)} fusion(bf16[8,4096,64]{1,2,0:T(8,128)(2,1)} %all-gather.5.cloned.1.call-done, bf16[48,4096]{1,0:T(8,128)(2,1)S(1)} %copy-done.1), kind=kOutput, calls=%fused_computation.2 | convolution fusion | flops 201326592 | bytes 4636672 | tf_op jit(solution)/shard_map/td,kdr->tkr/dot_general | solution.py:24
  151.2 0.2 fusion.3
  151.4 3.4 %psum.14 = bf16[48,64]{1,0:T(8,128)(2,1)S(1)} all-reduce(f32[48,64]{1,0:T(8,128)S(1)} %bitcast.17), channel_id=1, replica_groups=mesh['group'=2,'adapter'=8,'tensor'=2] {'tensor'}, use_global_device_ids=true, to_apply=%region_0.0 | all-reduce | flops 3072 | bytes 18432 | tf_op jit(solution)/shard_map/psum | solution.py:29
  154.8 30.5 %all_gather.11 = bf16[384,64]{1,0:T(8,128)(2,1)S(1)} all-gather(bf16[48,64]{1,0:T(8,128)(2,1)S(1)} %psum.14), channel_id=1, replica_groups=mesh['group'=2,'adapter'=8,'tensor'=2] {'adapter'}, dimensions={0}, use_global_device_ids=true | all-gather | bytes 55296 | tf_op jit(solution)/shard_map/all_gather | solution.py:30
  185.4 0.1 constant_dynamic-slice_fusion
  185.5 0.1 copy.6
  185.6 0.0 copy-done
  185.6 1.8 fusion
  187.4 8.0 %all-reduce.1 = bf16[384,1024]{1,0:T(8,128)(2,1)} all-reduce(f32[384,1024]{1,0:T(8,128)S(1)} %fusion), channel_id=1, replica_groups=mesh['group'=2,'adapter'=8,'tensor'=2] {'tensor'}, use_global_device_ids=true, to_apply=%region_1.0 | all-reduce | flops 393216 | bytes 2359296 | tf_op jit(solution)/shard_map/psum | solution.py:46
  (1 shorter events, 0.0 us)
Async XLA Ops:
  6.5 179.0 %copy-start = (bf16[8,32,1024]{2,1,0:T(8,128)(2,1)S(1)}, bf16[8,32,1024]{2,1,0:T(8,128)(2,1)}, u32[]{:S(2)}) copy-start(bf16[8,32,1024]{2,1,0:T(8,128)(2,1)} %param.9) | copy-start | bytes 1572868
  6.5 66.2 %all-gather.3.cloned.1.call-start = ((), (), s32[]{:S(2)}) async-start(), calls=%async_computation | async-start | bytes 3538944 | tf_op jit(solution)/shard_map/all_gather | solution.py:17
  7.3 139.7 %all-gather.5.cloned.1.call-start = ((), (), s32[]{:S(2)}) async-start(), calls=%async_computation.1 | async-start | bytes 4718592 | tf_op jit(solution)/shard_map/all_gather | solution.py:22
  9.6 137.4 %copy-start.1 = (bf16[48,4096]{1,0:T(8,128)(2,1)S(1)}, bf16[48,4096]{1,0:T(8,128)(2,1)}, u32[]{:S(2)}) copy-start(bf16[48,4096]{1,0:T(8,128)(2,1)} %param.5) | copy-start | bytes 1179652
Sparse Core Ops, SparseCore 0:
  9.5 63.1 all-gather.2
  74.9 72.0 all-gather.4
where the time goes:
time: 202 us
  waiting for transfers between devices  130 us (64%)
  blocking collectives  42 us (21%)
  matrix products  15.2 us (8%)
  between operations  13.5 us (7%)
    all_gather x1, waiting for transfers between devices, local(): row_slice = lax.all_gather(down_weight, 'adapter', axis=0, tiled=True)  65.2 us
    all_gather x1, waiting for transfers between devices, local(): lax.all_gather(tokens, 'adapter', axis=0, tiled=True)  63.2 us
    all_gather x1, blocking collectives, local(): low = lax.all_gather(own_low, 'adapter', axis=0, tiled=True)  30.5 us
    dot_general x1, matrix products, local(): jnp.dot(lax.all_gather(tokens, 'adapter', axis=0, tiled=True), output_wei...  8.98 us
    psum x1, blocking collectives, local(): summed = lax.psum(partial_output, 'tensor')  7.99 us
    dot_general x1, matrix products, local(): jnp.einsum('td,kdr->tkr', tokens, row_slice, preferred_element_type=jnp.f...  4.27 us
  transfers between devices with their start and end apart: 2, of which 2 were waited for; matrix products, arithmetic and copies ran while one was open for 5% of the time, Pallas kernels for 0%

commit v1 on v0

v1 whole, which is shorter than its diff:
```python
import functools

import jax
import jax.numpy as jnp
from jax import lax
from jax.experimental import pallas as pl
from jax.experimental.pallas import tpu as pltpu
from jax.sharding import PartitionSpec as P

adapter_scale = 2.0
CHUNK = 16
TILE = 256
MESH = pl.DeviceIdType.MESH


def when(condition, action):
    pl.when(condition)(action)


def kernel(
    count, wide, phases,
    x_hbm, ids_ref, w_hbm, down_hbm, up_hbm, out_ref,
    xs, w, down, up, part_out, part_in, base_out, base_in, lows,
    load_sem, own_sem,
    up_send, up_recv,
    right_send, left_send, line_recv,
    side_send, side_recv, cross_send, cross_recv,
    part_send, part_recv, base_send, base_recv, low_send, low_recv,
):
    deep = count // wide
    me = lax.axis_index("adapter")
    core = lax.axis_index("tensor")
    z, y = lax.div(me, wide), lax.rem(me, wide)
    features = x_hbm.shape[1]
    half = features // 2
    rank = down.shape[1]
    half_rank = rank // 2
    columns = w.shape[1]
    rows = count * CHUNK
    pack = rows // 2
    beside = z + 1 - 2 * lax.rem(z, 2)
    mirror = 1 - y

    def place(zz, yy):
        return zz * wide + yy

    def block(phase, a, first=0, size=features):
        return xs.at[phase, pl.ds(pl.multiple_of(a * CHUNK, CHUNK), CHUNK), pl.ds(first, size)]

    def own(phase):
        return x_hbm.at[pl.ds(phase * CHUNK, CHUNK), :]

    def remote(src, dst, send, recv, **device):
        return pltpu.make_async_remote_copy(
            src_ref=src, dst_ref=dst, send_sem=send, recv_sem=recv,
            device_id=device, device_id_type=MESH,
        )

    w_copy = pltpu.make_async_copy(w_hbm, w, load_sem.at[0])
    down_copy = pltpu.make_async_copy(down_hbm.at[0], down, load_sem.at[1])
    up_rows = pl.ds(pl.multiple_of(core * half_rank, half_rank), half_rank)
    up_copy = pltpu.make_async_copy(up_hbm, up.at[:, up_rows, :], load_sem.at[2])
    up_remote = remote(up_hbm, up.at[:, up_rows, :], up_send, up_recv, tensor=1 - core)

    def own_copy(phase):
        return pltpu.make_async_copy(own(phase), block(phase, me), own_sem.at[phase])

    w_copy.start()
    down_copy.start()
    up_copy.start()
    for phase in range(phases):
        own_copy(phase).start()

    barrier = pltpu.get_barrier_semaphore()
    pl.semaphore_signal(barrier, inc=1, device_id={"tensor": 1 - core}, device_id_type=MESH)
    for k in range(1, count):
        pl.semaphore_signal(
            barrier, inc=1, device_id={"adapter": lax.rem(me + k, count)}, device_id_type=MESH
        )
    pl.semaphore_wait(barrier, count)

    def right(phase, s, src=None):
        dst = block(phase, place(s, y))
        return remote(dst if src is None else src, dst, right_send.at[phase, s],
                      line_recv.at[phase, s], adapter=lax.rem(me + wide, count))

    def left(phase, s, src=None):
        dst = block(phase, place(s, y))
        return remote(dst if src is None else src, dst, left_send.at[phase, s],
                      line_recv.at[phase, s], adapter=lax.rem(me + count - wide, count))

    def side(phase, s, size, src=None):
        dst = block(phase, place(s, y), 0, size)
        return remote(dst if src is None else src, dst, side_send.at[phase, s],
                      side_recv.at[phase, s], adapter=place(z, mirror))

    def side_in(phase, s, size):
        dst = block(phase, place(s, mirror), 0, size)
        return remote(dst, dst, side_send.at[phase, s], side_recv.at[phase, s],
                      adapter=place(z, mirror))

    def cross(phase, s):
        dst = block(phase, place(s, mirror), half, half)
        return remote(dst, dst, cross_send.at[phase], cross_recv.at[phase],
                      adapter=place(beside, y))

    def by_size(s, action):
        when(s == beside, lambda: action(half))
        when(s != beside, lambda: action(features))

    def send_own(phase):
        when(z + 1 < deep, lambda: right(phase, z, own(phase)).start())
        when(z > 0, lambda: left(phase, z, own(phase)).start())
        if wide == 2:
            side(phase, z, features, own(phase)).start()

    def relay(phase, d):
        def pass_on(s):
            if wide == 2:
                by_size(s, lambda size: side(phase, s, size).start())

        def from_left():
            right(phase, z - d).wait_recv()
            when(z + 1 < deep, lambda: right(phase, z - d).start())
            pass_on(z - d)

        def from_right():
            left(phase, z + d).wait_recv()
            when(z > 0, lambda: left(phase, z + d).start())
            pass_on(z + d)

        when(z >= d, from_left)
        when(z + d < deep, from_right)

    def pass_across(phase):
        if wide == 2:
            side_in(phase, z, features).wait_recv()
            cross(phase, z).start()

    def finish(phase):
        own_copy(phase).wait()
        if wide == 2:
            for s in range(deep):
                when(z != s, lambda s=s: by_size(
                    s, lambda size: side_in(phase, s, size).wait_recv()))
            cross(phase, beside).wait_recv()

    def part_copy(phase):
        return remote(part_out.at[phase], part_in.at[phase], part_send.at[phase],
                      part_recv.at[phase], tensor=1 - core)

    def base_copy(phase):
        return remote(base_out.at[phase], base_in.at[phase], base_send.at[phase],
                      base_recv.at[phase], tensor=1 - core)

    def low_copy(phase, k):
        return remote(lows.at[phase, me], lows.at[phase, me], low_send.at[phase, k],
                      low_recv.at[phase, me], adapter=lax.rem(me + k, count))

    def low_in(phase, k):
        source = lax.rem(me + k, count)
        slot = lows.at[phase, source]
        return remote(slot, slot, low_send.at[phase, k], low_recv.at[phase, source],
                      adapter=source)

    def project_down(phase):
        ids = jnp.concatenate(
            [ids_ref[pl.ds((a * phases + phase) * CHUNK, CHUNK), :] for a in range(count)], axis=0
        )
        low = jnp.dot(xs[phase], down[...], preferred_element_type=jnp.float32)
        low = jnp.where(ids == me, low, 0.0)
        part_out[phase] = jnp.concatenate([low[:pack], low[pack:]], axis=1)
        part_copy(phase).start()

    def project(phase):
        @pl.loop(0, columns // TILE)
        def _(n):
            cols = pl.ds(pl.multiple_of(n * TILE, TILE), TILE)
            base_out[phase, :, cols] = jnp.dot(
                xs[phase], w[:, cols], preferred_element_type=jnp.float32
            )

        base_copy(phase).start()

    def share_low(phase):
        part_copy(phase).wait_recv()
        lows[phase, me] = (part_out[phase] + part_in[phase]).astype(jnp.bfloat16)
        for k in range(1, count):
            low_copy(phase, k).start()

    def write(phase):
        for k in range(1, count):
            low_in(phase, k).wait_recv()
        base_copy(phase).wait_recv()
        top = jnp.concatenate([lows[phase, a, :, :rank] for a in range(count)], axis=1)
        low_half = jnp.concatenate([lows[phase, a, :, rank:] for a in range(count)], axis=1)
        scattered = jnp.concatenate([top, low_half], axis=0)
        for n in range(columns // TILE):
            cols = pl.ds(n * TILE, TILE)
            delta = jnp.dot(
                scattered, up[:, :, cols].reshape(count * rank, TILE),
                preferred_element_type=jnp.float32,
            )
            total = base_out[phase, :, cols] + base_in[phase, :, cols] + adapter_scale * delta
            total = total.astype(jnp.bfloat16)
            for a in range(count):
                out_ref[pl.ds((a * phases + phase) * CHUNK, CHUNK), cols] = (
                    total[a * CHUNK:(a + 1) * CHUNK]
                )

    send_own(0)
    up_remote.start()
    for phase in range(phases):
        relay(phase, 1)
        pass_across(phase)
        if phase + 1 < phases:
            send_own(phase + 1)
        if phase == 1:
            down_copy.wait()
            w_copy.wait()
        if phase >= 1:
            project_down(phase - 1)
            project(phase - 1)
        for d in range(2, deep):
            relay(phase, d)
            if d == 2 and phase >= 1:
                share_low(phase - 1)
        finish(phase)
    if phases == 1:
        down_copy.wait()
        w_copy.wait()
    last = phases - 1
    project_down(last)
    up_copy.wait()
    up_remote.wait_recv()
    project(last)
    share_low(last)
    for phase in range(phases):
        write(phase)

    up_remote.wait_send()
    for phase in range(phases):
        part_copy(phase).wait_send()
        base_copy(phase).wait_send()
        for k in range(1, count):
            low_copy(phase, k).wait_send()
        for s in range(deep):
            when(jnp.logical_and(z >= s, z + 1 < deep),
                 lambda s=s: right(phase, s).wait_send())
            when(jnp.logical_and(z <= s, z > 0),
                 lambda s=s: left(phase, s).wait_send())
            if wide == 2:
                by_size(s, lambda size, s=s: side(phase, s, size).wait_send())
        if wide == 2:
            cross(phase, z).wait_send()


def local(count, wide, tokens, token_row_adapter, output_weight, down_weight, up_weight):
    own_rows, features = tokens.shape
    total_rows = token_row_adapter.shape[0]
    columns = output_weight.shape[1]
    rank = down_weight.shape[2]
    phases = own_rows // CHUNK
    deep = count // wide
    rows = count * CHUNK
    dma = pltpu.SemaphoreType.DMA
    anywhere = pl.BlockSpec(memory_space=pl.ANY)
    vmem = pl.BlockSpec(memory_space=pltpu.VMEM)
    return pl.pallas_call(
        functools.partial(kernel, count, wide, phases),
        out_shape=jax.ShapeDtypeStruct((total_rows, columns), jnp.bfloat16),
        in_specs=[anywhere, vmem, anywhere, anywhere, anywhere],
        out_specs=vmem,
        scratch_shapes=[
            pltpu.VMEM((phases, rows, features), jnp.bfloat16),
            pltpu.VMEM((features, columns), jnp.bfloat16),
            pltpu.VMEM((features, rank), jnp.bfloat16),
            pltpu.VMEM((count, rank, columns), jnp.bfloat16),
            pltpu.VMEM((phases, rows // 2, 2 * rank), jnp.float32),
            pltpu.VMEM((phases, rows // 2, 2 * rank), jnp.float32),
            pltpu.VMEM((phases, rows, columns), jnp.float32),
            pltpu.VMEM((phases, rows, columns), jnp.float32),
            pltpu.VMEM((phases, count, rows // 2, 2 * rank), jnp.bfloat16),
            dma((3,)), dma((phases,)),
            dma, dma,
            dma((phases, deep)), dma((phases, deep)), dma((phases, deep)),
            dma((phases, deep)), dma((phases, deep)), dma((phases,)), dma((phases,)),
            dma((phases,)), dma((phases,)), dma((phases,)), dma((phases,)),
            dma((phases, count)), dma((phases, count)),
        ],
        compiler_params=pltpu.CompilerParams(
            collective_id=0, has_side_effects=True, vmem_limit_bytes=48 << 20
        ),
    )(tokens, token_row_adapter, output_weight, down_weight, up_weight)


def solution(mesh):
    count = mesh.shape["adapter"]
    wide = 2 if count == 8 else 1
    placed = (
        P(("group", "adapter"), "tensor"),
        P("group", None),
        P("tensor", "adapter"),
        P(("group", "adapter"), "tensor", None),
        P("group", "tensor", "adapter"),
    )
    return jax.shard_map(
        functools.partial(local, count, wide),
        mesh=mesh, in_specs=placed, out_specs=P("group", "adapter"), check_vma=False,
    )
```

time: 202 us -> 61.3 us (0.30)
  waiting for transfers between devices: 130 us -> 0 us
  Pallas kernels: 0 us -> 55.8 us
  blocking collectives: 42 us -> 0 us
  matrix products: 15.2 us -> 0 us
  between operations: 13.5 us -> 0.03 us
  local copies, waits for them, and re-layouts: 0.94 us -> 5.25 us
    all_gather x2 -> x0, waiting for transfers between devices: 128 us -> none  [the longest x1 65.2 us: local(): row_slice = lax.all_gather(down_weight, 'adapter', axis=0, tiled=True)]
    pallas_call x0 -> x1, Pallas kernels: none -> 55.8 us  [local(): pl.pallas_call(functools.partial(kernel, count, wide, phases), out_shape=...]
    all_gather x1 -> x0, blocking collectives: 30.5 us -> none  [local(): low = lax.all_gather(own_low, 'adapter', axis=0, tiled=True)]
    dot_general x4 -> x0, matrix products: 15.2 us -> none  [the longest x1 8.98 us: local(): jnp.dot(lax.all_gather(tokens, 'adapter', axis=0, tiled=True), output_wei...]
    psum x2 -> x0, blocking collectives: 11.4 us -> none  [the longest x1 7.99 us: local(): summed = lax.psum(partial_output, 'tensor')]
    unnamed x4 -> x7, local copies, waits for them, and re-layouts: 0.01 us -> 5.25 us
  transfers between devices with their start and end apart: 2 -> 0, of which waited for: 2 -> 0; matrix products, arithmetic and copies ran while one was open for 5% -> 0% of each run, Pallas kernels for 0% -> 0%
where the time goes in v1:
time: 61.3 us; the launch traced here: 61.1 us
  Pallas kernels  55.8 us (91%)
  local copies, waits for them, and re-layouts  5.25 us (9%)
    pallas_call x1, Pallas kernels, local(): pl.pallas_call(functools.partial(kernel, count, wide, phases), out_shape=...  55.8 us
    unnamed x7, local copies, waits for them, and re-layouts  5.25 us

profile of v1, /device:TPU:0, one launch (start us, length us, event | category | flops | bytes accessed | tf_op | source)
XLA Modules:
  0.0 61.1 jit_solution(17674732604983398588)
XLA Ops:
  0.0 0.8 %copy.6.ids_ref = s32[384,1]{1,0:T(8,128)S(1)} copy(s32[384,1]{0,1:T(1,128)} %param.6) | data formatting | bytes 3072 | tf_op args[1]
  0.8 1.5 %copy.7.down_hbm = bf16[1,4096,64]{2,1,0:T(8,128)(2,1)S(1)} copy(bf16[1,4096,64]{1,2,0:T(8,128)(2,1)} %param.8) | data formatting | bytes 1048576 | tf_op args[3]
  2.3 0.0 copy-start
  2.4 1.0 %copy-done = bf16[8,32,1024]{2,1,0:T(8,128)(2,1)S(1)} copy-done((bf16[8,32,1024]{2,1,0:T(8,128)(2,1)S(1)}, bf16[8,32,1024]{2,1,0:T(8,128)(2,1)}, u32[]{:S(2)}) %copy-start) | copy-done | bytes 524312
  3.4 0.0 copy-start.1
  3.4 1.0 %copy-done.1 = bf16[48,4096]{1,0:T(8,128)(2,1)S(1)} copy-done((bf16[48,4096]{1,0:T(8,128)(2,1)S(1)}, bf16[48,4096]{1,0:T(8,128)(2,1)}, u32[]{:S(2)}) %copy-start.1) | copy-done | bytes 393240
  4.4 55.8 %shard_map.55 = bf16[384,1024]{1,0:T(8,128)(2,1)S(1)} custom-call(bf16[48,4096]{1,0:T(8,128)(2,1)S(1)} %copy-done.1, s32[384,1]{1,0:T(8,128)S(1)} %copy.6.ids_ref, bf16[4096,1024]{1,0:T(8,128)(2,1)} %w_hbm.1, bf16[1,4096,64]{2,1,0:T(8,128)(2,1)S(1)} %copy.7.down_hbm, bf16[8,32,1024]{2,1,0:T(8,128)(2,1)S(1)} %copy-done), custom_call_target="tpu_custom_call" | custom-call | tf_op jit(solution)/shard_map/pallas_call | solution.py:269
  60.2 0.9 %copy.9 = bf16[384,1024]{1,0:T(8,128)(2,1)} copy(bf16[384,1024]{1,0:T(8,128)(2,1)S(1)} %shard_map.55) | data formatting | bytes 1572864
Async XLA Ops:
  2.3 1.0 %copy-start = (bf16[8,32,1024]{2,1,0:T(8,128)(2,1)S(1)}, bf16[8,32,1024]{2,1,0:T(8,128)(2,1)}, u32[]{:S(2)}) copy-start(bf16[8,32,1024]{2,1,0:T(8,128)(2,1)} %up_hbm.1) | copy-start | bytes 1572868
  3.4 1.0 %copy-start.1 = (bf16[48,4096]{1,0:T(8,128)(2,1)S(1)}, bf16[48,4096]{1,0:T(8,128)(2,1)}, u32[]{:S(2)}) copy-start(bf16[48,4096]{1,0:T(8,128)(2,1)} %x_hbm.1) | copy-start | bytes 1179652

commit v2 on v1

--- a/solution.py
+++ b/solution.py
@@ -20,12 +20,12 @@
 def kernel(
     count, wide, phases,
     x_hbm, ids_ref, w_hbm, down_hbm, up_hbm, out_ref,
-    xs, w, down, up, part_out, part_in, base_out, base_in, lows,
+    xs, w, down, up, part_out, part_in, base_out, base_in, pair, lows,
     load_sem, own_sem,
     up_send, up_recv,
     right_send, left_send, line_recv,
     side_send, side_recv, cross_send, cross_recv,
-    part_send, part_recv, base_send, base_recv, low_send, low_recv,
+    part_send, part_recv, base_send, base_recv, pair_send, pair_recv, low_send, low_recv,
 ):
     deep = count // wide
     me = lax.axis_index("adapter")
@@ -33,11 +33,10 @@
     z, y = lax.div(me, wide), lax.rem(me, wide)
     features = x_hbm.shape[1]
     half = features // 2
-    rank = down.shape[1]
+    rank = down.shape[0]
     half_rank = rank // 2
     columns = w.shape[1]
     rows = count * CHUNK
-    pack = rows // 2
     beside = z + 1 - 2 * lax.rem(z, 2)
     mirror = 1 - y
 
@@ -73,11 +72,16 @@
 
     barrier = pltpu.get_barrier_semaphore()
     pl.semaphore_signal(barrier, inc=1, device_id={"tensor": 1 - core}, device_id_type=MESH)
-    for k in range(1, count):
+    for k in range(1, deep):
         pl.semaphore_signal(
-            barrier, inc=1, device_id={"adapter": lax.rem(me + k, count)}, device_id_type=MESH
-        )
-    pl.semaphore_wait(barrier, count)
+            barrier, inc=1, device_id={"adapter": lax.rem(me + k * wide, count)},
+            device_id_type=MESH,
+        )
+    if wide == 2:
+        pl.semaphore_signal(
+            barrier, inc=1, device_id={"adapter": place(z, mirror)}, device_id_type=MESH
+        )
+    pl.semaphore_wait(barrier, deep - 1 + wide)
 
     def right(phase, s, src=None):
         dst = block(phase, place(s, y))
@@ -153,23 +157,30 @@
         return remote(base_out.at[phase], base_in.at[phase], base_send.at[phase],
                       base_recv.at[phase], tensor=1 - core)
 
+    def pair_copy(phase):
+        return remote(pair.at[phase, 0], pair.at[phase, 1], pair_send.at[phase],
+                      pair_recv.at[phase], adapter=place(z, mirror))
+
     def low_copy(phase, k):
-        return remote(lows.at[phase, me], lows.at[phase, me], low_send.at[phase, k],
-                      low_recv.at[phase, me], adapter=lax.rem(me + k, count))
+        return remote(lows.at[phase, z], lows.at[phase, z], low_send.at[phase, k],
+                      low_recv.at[phase, z], adapter=lax.rem(me + k * wide, count))
 
     def low_in(phase, k):
-        source = lax.rem(me + k, count)
+        source = lax.rem(z + k, deep)
         slot = lows.at[phase, source]
         return remote(slot, slot, low_send.at[phase, k], low_recv.at[phase, source],
-                      adapter=source)
+                      adapter=place(source, y))
+
+    def phase_ids(phase):
+        return jnp.concatenate(
+            [ids_ref[:, pl.ds((a * phases + phase) * CHUNK, CHUNK)] for a in range(count)], axis=1
+        )
 
     def project_down(phase):
-        ids = jnp.concatenate(
-            [ids_ref[pl.ds((a * phases + phase) * CHUNK, CHUNK), :] for a in range(count)], axis=0
-        )
-        low = jnp.dot(xs[phase], down[...], preferred_element_type=jnp.float32)
-        low = jnp.where(ids == me, low, 0.0)
-        part_out[phase] = jnp.concatenate([low[:pack], low[pack:]], axis=1)
+        low = lax.dot_general(
+            down[...], xs[phase], (((1,), (1,)), ((), ())), preferred_element_type=jnp.float32
+        )
+        part_out[phase] = jnp.where(phase_ids(phase) == me, low, 0.0)
         part_copy(phase).start()
 
     def project(phase):
@@ -184,22 +195,36 @@
 
     def share_low(phase):
         part_copy(phase).wait_recv()
-        lows[phase, me] = (part_out[phase] + part_in[phase]).astype(jnp.bfloat16)
-        for k in range(1, count):
+        low = (part_out[phase] + part_in[phase]).astype(jnp.bfloat16)
+        if wide == 2:
+            pair[phase, 0] = low
+            pair_copy(phase).start()
+        else:
+            lows[phase, z] = low
+
+    def spread_low(phase):
+        if wide == 2:
+            pair_copy(phase).wait_recv()
+            lows[phase, z] = pair[phase, 0] + pair[phase, 1]
+        for k in range(1, deep):
             low_copy(phase, k).start()
 
     def write(phase):
-        for k in range(1, count):
+        for k in range(1, deep):
             low_in(phase, k).wait_recv()
         base_copy(phase).wait_recv()
-        top = jnp.concatenate([lows[phase, a, :, :rank] for a in range(count)], axis=1)
-        low_half = jnp.concatenate([lows[phase, a, :, rank:] for a in range(count)], axis=1)
-        scattered = jnp.concatenate([top, low_half], axis=0)
+        low = lows[phase, 0].astype(jnp.float32)
+        for s in range(1, deep):
+            low += lows[phase, s].astype(jnp.float32)
+        ids = phase_ids(phase)
+        scattered = jnp.concatenate(
+            [jnp.where(ids == a, low, 0.0).astype(jnp.bfloat16) for a in range(count)], axis=0
+        )
         for n in range(columns // TILE):
             cols = pl.ds(n * TILE, TILE)
-            delta = jnp.dot(
+            delta = lax.dot_general(
                 scattered, up[:, :, cols].reshape(count * rank, TILE),
-                preferred_element_type=jnp.float32,
+                (((0,), (0,)), ((), ())), preferred_element_type=jnp.float32,
             )
             total = base_out[phase, :, cols] + base_in[phase, :, cols] + adapter_scale * delta
             total = total.astype(jnp.bfloat16)
@@ -225,24 +250,35 @@
             relay(phase, d)
             if d == 2 and phase >= 1:
                 share_low(phase - 1)
+        if phase >= 1:
+            spread_low(phase - 1)
+        if phase == 1:
+            up_copy.wait()
+            up_remote.wait_recv()
+        if phase >= 2:
+            write(phase - 2)
         finish(phase)
     if phases == 1:
         down_copy.wait()
         w_copy.wait()
     last = phases - 1
     project_down(last)
-    up_copy.wait()
-    up_remote.wait_recv()
+    if last == 0:
+        up_copy.wait()
+        up_remote.wait_recv()
+    share_low(last)
     project(last)
-    share_low(last)
-    for phase in range(phases):
+    spread_low(last)
+    for phase in range(max(last - 1, 0), phases):
         write(phase)
 
     up_remote.wait_send()
     for phase in range(phases):
         part_copy(phase).wait_send()
         base_copy(phase).wait_send()
-        for k in range(1, count):
+        if wide == 2:
+            pair_copy(phase).wait_send()
+        for k in range(1, deep):
             low_copy(phase, k).wait_send()
         for s in range(deep):
             when(jnp.logical_and(z >= s, z + 1 < deep),
@@ -264,34 +300,36 @@
     deep = count // wide
     rows = count * CHUNK
     dma = pltpu.SemaphoreType.DMA
-    anywhere = pl.BlockSpec(memory_space=pl.ANY)
+    hbm = pl.BlockSpec(memory_space=pltpu.HBM)
     vmem = pl.BlockSpec(memory_space=pltpu.VMEM)
     return pl.pallas_call(
         functools.partial(kernel, count, wide, phases),
         out_shape=jax.ShapeDtypeStruct((total_rows, columns), jnp.bfloat16),
-        in_specs=[anywhere, vmem, anywhere, anywhere, anywhere],
+        in_specs=[hbm, vmem, hbm, hbm, hbm],
         out_specs=vmem,
         scratch_shapes=[
             pltpu.VMEM((phases, rows, features), jnp.bfloat16),
             pltpu.VMEM((features, columns), jnp.bfloat16),
-            pltpu.VMEM((features, rank), jnp.bfloat16),
+            pltpu.VMEM((rank, features), jnp.bfloat16),
             pltpu.VMEM((count, rank, columns), jnp.bfloat16),
-            pltpu.VMEM((phases, rows // 2, 2 * rank), jnp.float32),
-            pltpu.VMEM((phases, rows // 2, 2 * rank), jnp.float32),
+            pltpu.VMEM((phases, rank, rows), jnp.float32),
+            pltpu.VMEM((phases, rank, rows), jnp.float32),
             pltpu.VMEM((phases, rows, columns), jnp.float32),
             pltpu.VMEM((phases, rows, columns), jnp.float32),
-            pltpu.VMEM((phases, count, rows // 2, 2 * rank), jnp.bfloat16),
+            pltpu.VMEM((phases, 2, rank, rows), jnp.bfloat16),
+            pltpu.VMEM((phases, deep, rank, rows), jnp.bfloat16),
             dma((3,)), dma((phases,)),
             dma, dma,
             dma((phases, deep)), dma((phases, deep)), dma((phases, deep)),
             dma((phases, deep)), dma((phases, deep)), dma((phases,)), dma((phases,)),
             dma((phases,)), dma((phases,)), dma((phases,)), dma((phases,)),
-            dma((phases, count)), dma((phases, count)),
+            dma((phases,)), dma((phases,)), dma((phases, deep)), dma((phases, deep)),
         ],
         compiler_params=pltpu.CompilerParams(
-            collective_id=0, has_side_effects=True, vmem_limit_bytes=48 << 20
+            collective_id=0, has_side_effects=True, vmem_limit_bytes=63 << 20
         ),
-    )(tokens, token_row_adapter, output_weight, down_weight, up_weight)
+    )(tokens, token_row_adapter.reshape(1, total_rows), output_weight,
+      jnp.swapaxes(down_weight, 1, 2), up_weight)
 
 
 def solution(mesh):

time: 61.3 us -> 56.3 us (0.918)
  local copies, waits for them, and re-layouts: 5.25 us -> 2.06 us
  Pallas kernels: 55.8 us -> 54 us
    unnamed x7 -> x1, local copies, waits for them, and re-layouts: 5.25 us -> 2.06 us
    pallas_call x1, Pallas kernels: 55.8 us -> 54 us  [local(): pl.pallas_call(functools.partial(kernel, count, wide, phases), out_shape=...]
where the time goes in v2:
time: 56.3 us; the launch traced here: 56.1 us
  Pallas kernels  54 us (96%)
  local copies, waits for them, and re-layouts  2.06 us (4%)
    pallas_call x1, Pallas kernels, local(): pl.pallas_call(functools.partial(kernel, count, wide, phases), out_shape=...  54 us
    unnamed x1, local copies, waits for them, and re-layouts  2.06 us

profile of v2, /device:TPU:0, one launch (start us, length us, event | category | flops | bytes accessed | tf_op | source)
XLA Modules:
  0.0 56.1 jit_solution(14292365004467990176)
XLA Ops:
  0.0 54.0 %shard_map.55 = bf16[384,1024]{1,0:T(8,128)(2,1)} custom-call(bf16[48,4096]{1,0:T(8,128)(2,1)} %x_hbm.1, s32[1,384]{1,0:T(1,128)} %bitcast.3, bf16[4096,1024]{1,0:T(8,128)(2,1)} %w_hbm.1, bf16[1,64,4096]{2,1,0:T(8,128)(2,1)} %bitcast.2, bf16[8,32,1024]{2,1,0:T(8,128)(2,1)} %up_hbm.1), custom_call_target="tpu_custom_call" | custom-call | tf_op jit(solution)/shard_map/pallas_call | solution.py:305
  54.0 2.1 %copy.7 = bf16[384,1024]{1,0:T(8,128)(2,1)} copy(bf16[384,1024]{1,0:T(8,128)(2,1)} %shard_map.55) | data formatting | bytes 1572864

commit v3 on v2

--- a/solution.py
+++ b/solution.py
@@ -9,6 +9,7 @@
 
 adapter_scale = 2.0
 CHUNK = 16
+PARTS = 2
 TILE = 256
 MESH = pl.DeviceIdType.MESH
 
@@ -32,7 +33,7 @@
     core = lax.axis_index("tensor")
     z, y = lax.div(me, wide), lax.rem(me, wide)
     features = x_hbm.shape[1]
-    half = features // 2
+    width = features // PARTS
     rank = down.shape[0]
     half_rank = rank // 2
     columns = w.shape[1]
@@ -43,11 +44,12 @@
     def place(zz, yy):
         return zz * wide + yy
 
-    def block(phase, a, first=0, size=features):
-        return xs.at[phase, pl.ds(pl.multiple_of(a * CHUNK, CHUNK), CHUNK), pl.ds(first, size)]
-
-    def own(phase):
-        return x_hbm.at[pl.ds(phase * CHUNK, CHUNK), :]
+    def block(phase, a, part):
+        return xs.at[phase, pl.ds(pl.multiple_of(a * CHUNK, CHUNK), CHUNK),
+                     pl.ds(part * width, width)]
+
+    def own(phase, part):
+        return x_hbm.at[pl.ds(phase * CHUNK, CHUNK), pl.ds(part * width, width)]
 
     def remote(src, dst, send, recv, **device):
         return pltpu.make_async_remote_copy(
@@ -62,7 +64,11 @@
     up_remote = remote(up_hbm, up.at[:, up_rows, :], up_send, up_recv, tensor=1 - core)
 
     def own_copy(phase):
-        return pltpu.make_async_copy(own(phase), block(phase, me), own_sem.at[phase])
+        return pltpu.make_async_copy(
+            x_hbm.at[pl.ds(phase * CHUNK, CHUNK), :],
+            xs.at[phase, pl.ds(pl.multiple_of(me * CHUNK, CHUNK), CHUNK), :],
+            own_sem.at[phase],
+        )
 
     w_copy.start()
     down_copy.start()
@@ -83,70 +89,77 @@
         )
     pl.semaphore_wait(barrier, deep - 1 + wide)
 
-    def right(phase, s, src=None):
-        dst = block(phase, place(s, y))
-        return remote(dst if src is None else src, dst, right_send.at[phase, s],
-                      line_recv.at[phase, s], adapter=lax.rem(me + wide, count))
-
-    def left(phase, s, src=None):
-        dst = block(phase, place(s, y))
-        return remote(dst if src is None else src, dst, left_send.at[phase, s],
-                      line_recv.at[phase, s], adapter=lax.rem(me + count - wide, count))
-
-    def side(phase, s, size, src=None):
-        dst = block(phase, place(s, y), 0, size)
-        return remote(dst if src is None else src, dst, side_send.at[phase, s],
-                      side_recv.at[phase, s], adapter=place(z, mirror))
-
-    def side_in(phase, s, size):
-        dst = block(phase, place(s, mirror), 0, size)
-        return remote(dst, dst, side_send.at[phase, s], side_recv.at[phase, s],
+    def right(phase, s, part, src=None):
+        dst = block(phase, place(s, y), part)
+        return remote(dst if src is None else src, dst, right_send.at[phase, s, part],
+                      line_recv.at[phase, s, part], adapter=lax.rem(me + wide, count))
+
+    def left(phase, s, part, src=None):
+        dst = block(phase, place(s, y), part)
+        return remote(dst if src is None else src, dst, left_send.at[phase, s, part],
+                      line_recv.at[phase, s, part], adapter=lax.rem(me + count - wide, count))
+
+    def side(phase, s, part, src=None):
+        dst = block(phase, place(s, y), part)
+        return remote(dst if src is None else src, dst, side_send.at[phase, s, part],
+                      side_recv.at[phase, s, part], adapter=place(z, mirror))
+
+    def side_in(phase, s, part):
+        dst = block(phase, place(s, mirror), part)
+        return remote(dst, dst, side_send.at[phase, s, part], side_recv.at[phase, s, part],
                       adapter=place(z, mirror))
 
     def cross(phase, s):
-        dst = block(phase, place(s, mirror), half, half)
+        dst = block(phase, place(s, mirror), PARTS - 1)
         return remote(dst, dst, cross_send.at[phase], cross_recv.at[phase],
                       adapter=place(beside, y))
 
-    def by_size(s, action):
-        when(s == beside, lambda: action(half))
-        when(s != beside, lambda: action(features))
+    def unless_crossed(s, part, action):
+        if part == PARTS - 1:
+            when(s != beside, action)
+        else:
+            action()
 
     def send_own(phase):
-        when(z + 1 < deep, lambda: right(phase, z, own(phase)).start())
-        when(z > 0, lambda: left(phase, z, own(phase)).start())
-        if wide == 2:
-            side(phase, z, features, own(phase)).start()
+        for part in range(PARTS):
+            src = own(phase, part)
+            when(z + 1 < deep, lambda: right(phase, z, part, src).start())
+            when(z > 0, lambda: left(phase, z, part, src).start())
+            if wide == 2:
+                side(phase, z, part, src).start()
 
     def relay(phase, d):
-        def pass_on(s):
+        def pass_on(s, part):
             if wide == 2:
-                by_size(s, lambda size: side(phase, s, size).start())
-
-        def from_left():
-            right(phase, z - d).wait_recv()
-            when(z + 1 < deep, lambda: right(phase, z - d).start())
-            pass_on(z - d)
-
-        def from_right():
-            left(phase, z + d).wait_recv()
-            when(z > 0, lambda: left(phase, z + d).start())
-            pass_on(z + d)
-
-        when(z >= d, from_left)
-        when(z + d < deep, from_right)
+                unless_crossed(s, part, lambda: side(phase, s, part).start())
+
+        def from_left(part):
+            right(phase, z - d, part).wait_recv()
+            when(z + 1 < deep, lambda: right(phase, z - d, part).start())
+            pass_on(z - d, part)
+
+        def from_right(part):
+            left(phase, z + d, part).wait_recv()
+            when(z > 0, lambda: left(phase, z + d, part).start())
+            pass_on(z + d, part)
+
+        for part in range(PARTS):
+            when(z >= d, lambda: from_left(part))
+            when(z + d < deep, lambda: from_right(part))
 
     def pass_across(phase):
         if wide == 2:
-            side_in(phase, z, features).wait_recv()
+            for part in range(PARTS):
+                side_in(phase, z, part).wait_recv()
             cross(phase, z).start()
 
     def finish(phase):
         own_copy(phase).wait()
         if wide == 2:
             for s in range(deep):
-                when(z != s, lambda s=s: by_size(
-                    s, lambda size: side_in(phase, s, size).wait_recv()))
+                for part in range(PARTS):
+                    when(z != s, lambda: unless_crossed(
+                        s, part, lambda: side_in(phase, s, part).wait_recv()))
             cross(phase, beside).wait_recv()
 
     def part_copy(phase):
@@ -218,13 +231,13 @@
             low += lows[phase, s].astype(jnp.float32)
         ids = phase_ids(phase)
         scattered = jnp.concatenate(
-            [jnp.where(ids == a, low, 0.0).astype(jnp.bfloat16) for a in range(count)], axis=0
-        )
+            [jnp.where(ids == a, low, 0.0) for a in range(count)], axis=0
+        ).T.astype(jnp.bfloat16)
         for n in range(columns // TILE):
             cols = pl.ds(n * TILE, TILE)
-            delta = lax.dot_general(
+            delta = jnp.dot(
                 scattered, up[:, :, cols].reshape(count * rank, TILE),
-                (((0,), (0,)), ((), ())), preferred_element_type=jnp.float32,
+                preferred_element_type=jnp.float32,
             )
             total = base_out[phase, :, cols] + base_in[phase, :, cols] + adapter_scale * delta
             total = total.astype(jnp.bfloat16)
@@ -237,19 +250,23 @@
     up_remote.start()
     for phase in range(phases):
         relay(phase, 1)
-        pass_across(phase)
+        if phase + 1 < phases:
+            pass_across(phase)
         if phase + 1 < phases:
             send_own(phase + 1)
         if phase == 1:
             down_copy.wait()
             w_copy.wait()
         if phase >= 1:
+            finish(phase - 1)
             project_down(phase - 1)
             project(phase - 1)
         for d in range(2, deep):
             relay(phase, d)
             if d == 2 and phase >= 1:
                 share_low(phase - 1)
+        if phase + 1 == phases:
+            pass_across(phase)
         if phase >= 1:
             spread_low(phase - 1)
         if phase == 1:
@@ -257,11 +274,11 @@
             up_remote.wait_recv()
         if phase >= 2:
             write(phase - 2)
-        finish(phase)
     if phases == 1:
         down_copy.wait()
         w_copy.wait()
     last = phases - 1
+    finish(last)
     project_down(last)
     if last == 0:
         up_copy.wait()
@@ -281,12 +298,13 @@
         for k in range(1, deep):
             low_copy(phase, k).wait_send()
         for s in range(deep):
-            when(jnp.logical_and(z >= s, z + 1 < deep),
-                 lambda s=s: right(phase, s).wait_send())
-            when(jnp.logical_and(z <= s, z > 0),
-                 lambda s=s: left(phase, s).wait_send())
-            if wide == 2:
-                by_size(s, lambda size, s=s: side(phase, s, size).wait_send())
+            for part in range(PARTS):
+                when(jnp.logical_and(z >= s, z + 1 < deep),
+                     lambda: right(phase, s, part).wait_send())
+                when(jnp.logical_and(z <= s, z > 0),
+                     lambda: left(phase, s, part).wait_send())
+                if wide == 2:
+                    unless_crossed(s, part, lambda: side(phase, s, part).wait_send())
         if wide == 2:
             cross(phase, z).wait_send()
 
@@ -320,8 +338,8 @@
             pltpu.VMEM((phases, deep, rank, rows), jnp.bfloat16),
             dma((3,)), dma((phases,)),
             dma, dma,
-            dma((phases, deep)), dma((phases, deep)), dma((phases, deep)),
-            dma((phases, deep)), dma((phases, deep)), dma((phases,)), dma((phases,)),
+            *[dma((phases, deep, PARTS)) for _ in range(5)],
+            dma((phases,)), dma((phases,)),
             dma((phases,)), dma((phases,)), dma((phases,)), dma((phases,)),
             dma((phases,)), dma((phases,)), dma((phases, deep)), dma((phases, deep)),
         ],

time: 56.3 us -> 54.7 us (0.972)
  Pallas kernels: 54 us -> 52.5 us
    pallas_call x1, Pallas kernels: 54 us -> 52.5 us  [local(): pl.pallas_call(functools.partial(kernel, count, wide, phases), out_shape=...]
where the time goes in v3:
time: 54.7 us; the launch traced here: 54.5 us
  Pallas kernels  52.5 us (96%)
  local copies, waits for them, and re-layouts  2.06 us (4%)
    pallas_call x1, Pallas kernels, local(): pl.pallas_call(functools.partial(kernel, count, wide, phases), out_shape=...  52.5 us
    unnamed x1, local copies, waits for them, and re-layouts  2.06 us

profile of v3, /device:TPU:0, one launch (start us, length us, event | category | flops | bytes accessed | tf_op | source)
XLA Modules:
  0.0 54.5 jit_solution(15403964864649780024)
XLA Ops:
  0.0 52.5 %shard_map.55 = bf16[384,1024]{1,0:T(8,128)(2,1)} custom-call(bf16[48,4096]{1,0:T(8,128)(2,1)} %x_hbm.1, s32[1,384]{1,0:T(1,128)} %bitcast.3, bf16[4096,1024]{1,0:T(8,128)(2,1)} %w_hbm.1, bf16[1,64,4096]{2,1,0:T(8,128)(2,1)} %bitcast.2, bf16[8,32,1024]{2,1,0:T(8,128)(2,1)} %up_hbm.1), custom_call_target="tpu_custom_call" | custom-call | tf_op jit(solution)/shard_map/pallas_call | solution.py:323
  52.5 2.1 %copy.7 = bf16[384,1024]{1,0:T(8,128)(2,1)} copy(bf16[384,1024]{1,0:T(8,128)(2,1)} %shard_map.55) | data formatting | bytes 1572864
